TPU v7x, 32 devices: a whole 2x2x4 slice. The times are simulated.
32 devices in a mesh: batch: 4 (over y, core), group: 2 (over x), ctx: 4 (over z).
Axes of the slice: x: 2, y: 2, z: 4, core: 2. Of those that a mesh axis runs over, the one named last changes fastest.
Arguments:
- block_input: bfloat16 [16, 2048, 1024], P(('batch', 'group'), 'ctx'), may hold values from -6 to 6
- doc_ids: int32 [16, 2048], P(('batch', 'group')), may hold values from 0 to 1, as said below
- out_cotangent: bfloat16 [16, 2048, 1024], P(('batch', 'group'), 'ctx'), may hold values from -6 to 6
- inward_weight: float32 [1024, 3072], P(None, 'group'), may hold values from -0.25 to 0.25
- inward_moment: float32 [1024, 3072], P(None, 'group')
- inward_square: float32 [1024, 3072], P(None, 'group'), as said below
- outward_weight: float32 [1024, 1024], P(None, 'group'), may hold values from -0.75 to 0.75
- outward_moment: float32 [1024, 1024], P(None, 'group')
- outward_square: float32 [1024, 1024], P(None, 'group'), as said below
- expand_weight: float32 [1024, 4096], P(None, 'group'), may hold values from -0.1875 to 0.1875
- expand_moment: float32 [1024, 4096], P(None, 'group')
- expand_square: float32 [1024, 4096], P(None, 'group'), as said below
- shrink_weight: float32 [4096, 1024], P(None, 'group'), may hold values from -0.09375 to 0.09375
- shrink_moment: float32 [4096, 1024], P(None, 'group')
- shrink_square: float32 [4096, 1024], P(None, 'group'), as said below
- vector_weight: float32 [13, 1024], P(None, 'group')
- vector_moment: float32 [13, 1024], P(None, 'group')
- vector_square: float32 [13, 1024], P(None, 'group'), as said below
Outputs:
- block_output: bfloat16 [16, 2048, 1024], P(('batch', 'group'), 'ctx')
- input_grad: float32 [16, 2048, 1024], P(('batch', 'group'), 'ctx')
- inward_master: float32 [1024, 3072], P(None, 'group')
- inward_first: float32 [1024, 3072], P(None, 'group')
- inward_second: float32 [1024, 3072], P(None, 'group')
- outward_master: float32 [1024, 1024], P(None, 'group')
- outward_first: float32 [1024, 1024], P(None, 'group')
- outward_second: float32 [1024, 1024], P(None, 'group')
- expand_master: float32 [1024, 4096], P(None, 'group')
- expand_first: float32 [1024, 4096], P(None, 'group')
- expand_second: float32 [1024, 4096], P(None, 'group')
- shrink_master: float32 [4096, 1024], P(None, 'group')
- shrink_first: float32 [4096, 1024], P(None, 'group')
- shrink_second: float32 [4096, 1024], P(None, 'group')
- vector_master: float32 [13, 1024], P(None, 'group')
- vector_first: float32 [13, 1024], P(None, 'group')
- vector_second: float32 [13, 1024], P(None, 'group')
Inputs may be any that keep to these rules, and one draw needn't show every extreme that they name: `doc_ids`: each sequence is document 0 up to a cut and document 1 from it on, both nonempty; in every aligned block of 2 sequences one sequence has its cut within its last 512 positions. `inward_square`: entries are positive. `outward_square`: entries are positive. `expand_square`: entries are positive. `shrink_square`: entries are positive. `vector_square`: entries are positive.
All inputs are finite; a program needn't handle non-finite values.
Results may differ from a plain program's by a relative error of at most 0.012.
The roundings to bfloat16 on the way count: a program that leaves them out, or rounds other values in their place, can miss the bound.
Values may be sent and summed in bfloat16 or wider, within the bound.
A program may use at most 704 MiB of HBM per device.

v0:
```python
import math

import jax
import jax.numpy as jnp
from jax import lax
from jax.sharding import PartitionSpec as P

HEADS = 16
ROTARY = 16
STEP = 10


norm_eps = 1e-05
adam_eps = 1e-08
first_decay = 0.9
second_decay = 0.95
decay_rate = 0.01
matrix_rate = 0.1
vector_rate = 0.8
neg_fill = -1e30


def layer_norm(values, norm_gain, norm_shift):
    row_mean = jnp.mean(values, -1, keepdims=True)
    centred = values - row_mean
    variance = jnp.mean(centred * centred, -1, keepdims=True)
    return centred * lax.rsqrt(variance + norm_eps) * norm_gain + norm_shift


def rotary_tables(positions, rot_dims):
    half_rot = rot_dims // 2
    frequency = jnp.exp(
        jnp.arange(half_rot).astype(jnp.float32) * (-2.0 * math.log(10000.0) / rot_dims)
    )
    angles = positions[:, None] * frequency[None, :]
    angles = jnp.concatenate([angles, angles], -1)
    return (jnp.cos(angles), jnp.sin(angles))


def rotate(values, cosine_table, sine_table):
    rot_dims = cosine_table.shape[-1]
    half_rot = rot_dims // 2
    rot_part = values[..., :rot_dims]
    lower_half = rot_part[..., :half_rot]
    upper_half = rot_part[..., half_rot:]
    turned = jnp.concatenate([-upper_half, lower_half], -1)
    spun = rot_part * cosine_table[:, None, :] + turned * sine_table[:, None, :]
    return jnp.concatenate([spun, values[..., rot_dims:]], -1)


def gelu_exact(values):
    return jax.nn.gelu(values, approximate=False)


def head_scores(query_part, key_part, allowed, score_scale):
    raw_scores = (
        jnp.einsum("sqhe,skhe->shqk", query_part, key_part, preferred_element_type=jnp.float32)
        * score_scale
    )
    return jnp.where(allowed[:, None], raw_scores, neg_fill)


def adam_step(weight, moment, square, gradient, rate):
    first = first_decay * moment + (1.0 - first_decay) * gradient
    second = second_decay * square + (1.0 - second_decay) * gradient * gradient
    first_hat = first / (1.0 - first_decay**STEP)
    second_hat = second / (1.0 - second_decay**STEP)
    master = weight - rate * (first_hat / (jnp.sqrt(second_hat) + adam_eps) + decay_rate * weight)
    return (master, first, second)


def update_all(weights, moments, squares, gradients):
    rates = (matrix_rate, matrix_rate, matrix_rate, matrix_rate, vector_rate)
    results = ()
    for place in range(5):
        results = results + adam_step(
            weights[place], moments[place], squares[place], gradients[place], rates[place]
        )
    return results


def local(
    block_input,
    doc_ids,
    out_cotangent,
    inward_weight,
    inward_moment,
    inward_square,
    outward_weight,
    outward_moment,
    outward_square,
    expand_weight,
    expand_moment,
    expand_square,
    shrink_weight,
    shrink_moment,
    shrink_square,
    vector_weight,
    vector_moment,
    vector_square,
):
    gathered = (
        lax.all_gather(inward_weight.astype(jnp.bfloat16), "group", axis=1, tiled=True),
        lax.all_gather(outward_weight.astype(jnp.bfloat16), "group", axis=1, tiled=True),
        lax.all_gather(expand_weight.astype(jnp.bfloat16), "group", axis=1, tiled=True),
        lax.all_gather(shrink_weight.astype(jnp.bfloat16), "group", axis=1, tiled=True),
        lax.all_gather(vector_weight.astype(jnp.bfloat16), "group", axis=1, tiled=True),
    )
    inward_copy, outward_copy, expand_copy, shrink_copy, vector_copy = gathered
    vector_full = vector_copy.astype(jnp.float32)
    seq_count, tok_count, model_width = block_input.shape
    head_count = HEADS
    head_size = model_width // head_count
    seq_length = doc_ids.shape[1]
    ffn_rows = expand_copy.shape[1] // model_width
    row_count = seq_count * tok_count
    score_scale = head_size ** (-0.5)
    offset = lax.axis_index("ctx") * tok_count
    residual = block_input.astype(jnp.float32).reshape(row_count, model_width)
    normed_attn, attn_norm_back = jax.vjp(layer_norm, residual, vector_full[0], vector_full[1])
    normed_mlp, mlp_norm_back = jax.vjp(layer_norm, residual, vector_full[2], vector_full[3])
    attn_in = normed_attn.astype(jnp.bfloat16)
    mlp_in = normed_mlp.astype(jnp.bfloat16)
    joint_rows = jnp.dot(attn_in, inward_copy, preferred_element_type=jnp.float32) + vector_full[
        4:7
    ].reshape(-1)
    split_shape = (seq_count, tok_count, head_count, head_size)
    query_pre = joint_rows[:, :model_width].reshape(split_shape)
    key_pre = joint_rows[:, model_width : 2 * model_width].reshape(split_shape)
    value_pre = joint_rows[:, 2 * model_width :]
    positions = (offset + jnp.arange(tok_count)).astype(jnp.float32)
    cosine_table, sine_table = rotary_tables(positions, ROTARY)
    query_turned, query_back = jax.vjp(
        lambda values: rotate(values, cosine_table, sine_table), query_pre
    )
    key_turned, key_back = jax.vjp(lambda values: rotate(values, cosine_table, sine_table), key_pre)
    query_low = query_turned.astype(jnp.bfloat16)
    key_low = key_turned.astype(jnp.bfloat16).reshape(seq_count, tok_count, model_width)
    value_low = value_pre.astype(jnp.bfloat16).reshape(seq_count, tok_count, model_width)
    key_rows, value_rows = (
        lax.all_gather(key_low, "ctx", axis=1, tiled=True),
        lax.all_gather(value_low, "ctx", axis=1, tiled=True),
    )
    full_shape = (seq_count, seq_length, head_count, head_size)
    key_heads = key_rows.reshape(full_shape)
    value_heads = value_rows.reshape(full_shape)
    query_places = offset + jnp.arange(tok_count)
    causal = jnp.arange(seq_length)[None, :] <= query_places[:, None]
    own_docs = lax.dynamic_slice_in_dim(doc_ids, offset, tok_count, 1)
    allowed = causal[None] & (own_docs[:, :, None] == doc_ids[:, None, :])
    head_block = math.gcd(head_count, 8)
    starts = list(range(0, head_count, head_block))
    attended_parts, maxima, totals = ([], [], [])
    for first_head in starts:
        chosen = slice(first_head, first_head + head_block)
        scores = head_scores(query_low[:, :, chosen], key_heads[:, :, chosen], allowed, score_scale)
        row_top = jnp.max(scores, -1, keepdims=True)
        lifted = jnp.exp(scores - row_top)
        row_total = jnp.sum(lifted, -1, keepdims=True)
        attn_probs = (lifted / row_total).astype(jnp.bfloat16)
        attended_parts.append(
            jnp.einsum(
                "shqk,skhe->sqhe",
                attn_probs,
                value_heads[:, :, chosen],
                preferred_element_type=jnp.float32,
            )
        )
        maxima.append(row_top)
        totals.append(row_total)
    attn_low = (
        jnp.concatenate(attended_parts, 2).reshape(row_count, model_width).astype(jnp.bfloat16)
    )
    attn_out = jnp.dot(attn_low, outward_copy, preferred_element_type=jnp.float32) + vector_full[7]
    pre_act = jnp.dot(mlp_in, expand_copy, preferred_element_type=jnp.float32) + vector_full[
        8 : 8 + ffn_rows
    ].reshape(-1)
    activation, act_back = jax.vjp(gelu_exact, pre_act)
    act_low = activation.astype(jnp.bfloat16)
    mlp_out = (
        jnp.dot(act_low, shrink_copy, preferred_element_type=jnp.float32)
        + vector_full[8 + ffn_rows]
    )
    block_output = (
        (residual + attn_out + mlp_out)
        .astype(jnp.bfloat16)
        .reshape(seq_count, tok_count, model_width)
    )
    grad_low = out_cotangent.reshape(row_count, model_width)
    grad_out = grad_low.astype(jnp.float32)
    shrink_grad = jnp.dot(act_low.T, grad_low, preferred_element_type=jnp.float32)
    act_grad = jnp.dot(grad_low, shrink_copy.T, preferred_element_type=jnp.float32)
    pre_grad = act_back(act_grad)[0].astype(jnp.bfloat16)
    expand_grad = jnp.dot(mlp_in.T, pre_grad, preferred_element_type=jnp.float32)
    mlp_in_grad = jnp.dot(pre_grad, expand_copy.T, preferred_element_type=jnp.float32)
    outward_grad = jnp.dot(attn_low.T, grad_low, preferred_element_type=jnp.float32)
    attended_grad = (
        jnp.dot(grad_low, outward_copy.T, preferred_element_type=jnp.float32)
        .astype(jnp.bfloat16)
        .reshape(split_shape)
    )
    query_grads, key_grads, value_grads, weighted = ([], [], [], [])
    for block_place, first_head in enumerate(starts):
        chosen = slice(first_head, first_head + head_block)
        key_part = key_heads[:, :, chosen]
        value_part = value_heads[:, :, chosen]
        query_part = query_low[:, :, chosen]
        grad_part = attended_grad[:, :, chosen]
        scores = head_scores(query_part, key_part, allowed, score_scale)
        attn_probs = jnp.exp(scores - maxima[block_place]) / totals[block_place]
        prob_grad = jnp.einsum(
            "sqhe,skhe->shqk", grad_part, value_part, preferred_element_type=jnp.float32
        )
        row_weight = jnp.sum(attn_probs * prob_grad, -1, keepdims=True)
        score_grad = (attn_probs * (prob_grad - row_weight)).astype(jnp.bfloat16)
        query_grads.append(
            jnp.einsum("shqk,skhe->sqhe", score_grad, key_part, preferred_element_type=jnp.float32)
            * score_scale
        )
        weighted.append(row_weight)
        value_grads.append(
            jnp.einsum(
                "shqk,sqhe->skhe",
                attn_probs.astype(jnp.bfloat16),
                grad_part,
                preferred_element_type=jnp.float32,
            )
        )
        key_grads.append(
            jnp.einsum(
                "shqk,sqhe->skhe", score_grad, query_part, preferred_element_type=jnp.float32
            )
            * score_scale
        )
    key_grad_all = jnp.concatenate(key_grads, 2).reshape(seq_count, seq_length, model_width)
    value_grad_all = jnp.concatenate(value_grads, 2).reshape(seq_count, seq_length, model_width)
    key_grad_sum, value_grad_sum = (
        lax.psum_scatter(key_grad_all, "ctx", scatter_dimension=1, tiled=True),
        lax.psum_scatter(value_grad_all, "ctx", scatter_dimension=1, tiled=True),
    )
    query_grad = query_back(jnp.concatenate(query_grads, 2))[0]
    key_grad = key_back(key_grad_sum.reshape(split_shape))[0]
    joint_grad = jnp.concatenate(
        [
            query_grad.reshape(row_count, model_width),
            key_grad.reshape(row_count, model_width),
            value_grad_sum.reshape(row_count, model_width),
        ],
        -1,
    ).astype(jnp.bfloat16)
    inward_grad = jnp.dot(attn_in.T, joint_grad, preferred_element_type=jnp.float32)
    attn_in_grad = jnp.dot(joint_grad, inward_copy.T, preferred_element_type=jnp.float32)
    residual_attn, gain_attn, shift_attn = attn_norm_back(attn_in_grad)
    residual_mlp, gain_mlp, shift_mlp = mlp_norm_back(mlp_in_grad)
    input_grad = (grad_out + residual_attn + residual_mlp).reshape(
        seq_count, tok_count, model_width
    )
    joint_sum = jnp.sum(joint_grad.astype(jnp.float32), 0).reshape(3, model_width)
    out_sum = jnp.sum(grad_out, 0)
    pre_sum = jnp.sum(pre_grad.astype(jnp.float32), 0).reshape(ffn_rows, model_width)
    vector_grad = jnp.concatenate(
        [
            gain_attn[None],
            shift_attn[None],
            gain_mlp[None],
            shift_mlp[None],
            joint_sum,
            out_sum[None],
            pre_sum,
            out_sum[None],
        ],
        0,
    )
    masters = (inward_weight, outward_weight, expand_weight, shrink_weight, vector_weight)
    moments = (inward_moment, outward_moment, expand_moment, shrink_moment, vector_moment)
    squares = (inward_square, outward_square, expand_square, shrink_square, vector_square)
    owned_part = (
        lax.psum_scatter(inward_grad, "group", scatter_dimension=1, tiled=True),
        lax.psum_scatter(outward_grad, "group", scatter_dimension=1, tiled=True),
        lax.psum_scatter(expand_grad, "group", scatter_dimension=1, tiled=True),
        lax.psum_scatter(shrink_grad, "group", scatter_dimension=1, tiled=True),
        lax.psum_scatter(vector_grad, "group", scatter_dimension=1, tiled=True),
    )
    summed = lax.psum(
        (owned_part[0], owned_part[1], owned_part[2], owned_part[3], owned_part[4]),
        ("batch", "ctx"),
    )
    results = update_all(masters, moments, squares, summed)
    return (block_output, input_grad) + tuple(results)


def solution(mesh):
    placed = (
        P(("batch", "group"), "ctx", None),
        P(("batch", "group"), None),
        P(("batch", "group"), "ctx", None),
        P(None, "group"),
        P(None, "group"),
        P(None, "group"),
        P(None, "group"),
        P(None, "group"),
        P(None, "group"),
        P(None, "group"),
        P(None, "group"),
        P(None, "group"),
        P(None, "group"),
        P(None, "group"),
        P(None, "group"),
        P(None, "group"),
        P(None, "group"),
        P(None, "group"),
    )
    return jax.shard_map(
        local,
        mesh=mesh,
        in_specs=placed,
        out_specs=(
            P(("batch", "group"), "ctx", None),
            P(("batch", "group"), "ctx", None),
            P(None, "group"),
            P(None, "group"),
            P(None, "group"),
            P(None, "group"),
            P(None, "group"),
            P(None, "group"),
            P(None, "group"),
            P(None, "group"),
            P(None, "group"),
            P(None, "group"),
            P(None, "group"),
            P(None, "group"),
            P(None, "group"),
            P(None, "group"),
            P(None, "group"),
        ),
        check_vma=False,
    )
```

profile of v0, /device:TPU:0, one launch (start us, length us, event | category | flops | bytes accessed | tf_op | source)
XLA Modules:
  0.0 2377.1 jit_solution(14312892190536876173)
XLA Ops:
  7.3 5.0 convert_element_type.104
  15.1 5.3 all_gather.21
  26.3 69.2 %all-gather.7.cloned.1.call-done = bf16[1024,3072]{1,0:T(8,128)(2,1)} async-done(((bf16[1024,1536]{1,0:T(8,128)(2,1)}), bf16[1024,3072]{1,0:T(8,128)(2,1)}) %all-gather.7.cloned.1.call-update) | async-done | bytes 6291472 | tf_op jit(solution)/shard_map/all_gather | solution.py:103
  95.5 9.4 broadcast_add_fusion
  104.9 4.6 fusion.95
  112.1 5.3 copy.53
  117.4 6.6 reshape.276
  127.2 7.2 reshape.294
  134.4 6.0 copy.76
  143.8 13.0 fusion.96
  156.8 5.2 copy.77
  162.8 6.1 copy.78
  181.2 6.3 convert_element_type.114
  187.5 6.7 convert_element_type.116
  198.1 5.3 convolution_convert_fusion
  203.4 6.4 reshape.295
  219.1 6.6 slice.129
  225.8 4.5 copy.79
  230.2 97.1 %all-gather.11.cloned.1.call-done = bf16[2,2048,1024]{1,2,0:T(8,128)(2,1)} async-done(((bf16[2,512,1024]{1,2,0:T(8,128)(2,1)}), bf16[2,2048,1024]{1,2,0:T(8,128)(2,1)}) %all-gather.11.cloned.1.call-update) | async-done | bytes 8388624 | tf_op jit(solution)/shard_map/all_gather | solution.py:141
  327.3 27.5 %fusion.37 = f32[2,8,512,2048]{3,2,1,0:T(8,128)} fusion(bf16[2,2048,16,64]{1,3,2,0:T(8,128)(2,1)} %bitcast.214, bf16[2,512,16,48]{1,3,2,0:T(8,128)(2,1)S(1)} %copy.79, bf16[2,512,16,16]{1,3,2,0:T(8,128)(2,1)S(1)} %copy-done.28), kind=kOutput, calls=%fused_computation.74 | convolution fusion | flops 2151677952 | bytes 73400320 | tf_op jit(solution)/shard_map/sqhe,skhe->shqk/dot_general | solution.py:57
  354.9 25.8 %fusion.39 = f32[2,8,512,2048]{3,2,1,0:T(8,128)} fusion(bf16[2,2048,16,64]{1,3,2,0:T(8,128)(2,1)} %bitcast.215, bf16[2,512,16,48]{1,3,2,0:T(8,128)(2,1)} %copy-done.23, bf16[2,512,16,16]{1,3,2,0:T(8,128)(2,1)S(1)} %copy-done.28), kind=kOutput, calls=%fused_computation.76 | convolution fusion | flops 2151677952 | bytes 73400320 | tf_op jit(solution)/shard_map/sqhe,skhe->shqk/dot_general | solution.py:57
  380.6 69.3 %fusion.100 = (f32[2,8,512]{2,1,0:T(8,128)S(1)}, f32[2,8,512,2048]{3,2,1,0:T(8,128)}) fusion(f32[2,8,512,2048]{3,2,1,0:T(8,128)} %fusion.37, pred[2,512,2048]{2,1,0:T(8,128)(4,1)S(1)} %copy-done.17), kind=kOutput, calls=%fused_computation.177 | output fusion | flops 100665344 | bytes 136347648 | tf_op jit(solution)/shard_map/sub | solution.py:158
  449.9 74.3 %fusion.101 = (f32[2,8,512]{2,1,0:T(8,128)S(1)}, f32[2,8,512,2048]{3,2,1,0:T(8,128)}) fusion(f32[2,8,512,2048]{3,2,1,0:T(8,128)} %fusion.39, pred[2,512,2048]{2,1,0:T(8,128)(4,1)S(1)} %copy-done.17), kind=kOutput, calls=%fused_computation.178 | output fusion | flops 100665344 | bytes 136347648 | tf_op jit(solution)/shard_map/sub | solution.py:158
  524.3 25.9 %fusion.30 = f32[2,2048,8,64]{1,3,2,0:T(8,128)} fusion(bf16[2,512,8,64]{1,3,2,0:T(8,128)(2,1)S(1)} %copy-done.27, f32[2,8,512,2048]{3,2,1,0:T(8,128)} %get-tuple-element.85, f32[2,8,512]{2,1,0:T(8,128)S(1)} %get-tuple-element.84), kind=kOutput, calls=%fused_computation.69 | convolution fusion | flops 2181038080 | bytes 76578816 | tf_op jit(solution)/shard_map/shqk,sqhe->skhe/dot_general | solution.py:222
  550.2 25.8 %fusion.27 = f32[2,2048,8,64]{1,3,2,0:T(8,128)} fusion(bf16[2,512,8,64]{1,3,2,0:T(8,128)(2,1)S(1)} %copy-done.25, f32[2,8,512,2048]{3,2,1,0:T(8,128)} %get-tuple-element.87, f32[2,8,512]{2,1,0:T(8,128)S(1)} %get-tuple-element.86), kind=kOutput, calls=%fused_computation.68 | convolution fusion | flops 2181038080 | bytes 76578816 | tf_op jit(solution)/shard_map/shqk,sqhe->skhe/dot_general | solution.py:222
  576.0 11.8 pad_maximum_fusion.1
  587.8 18.9 copy.65
  606.7 11.6 copy.47
  618.3 44.4 %multiply_reduce_fusion = (f32[2,8,512]{2,1,0:T(8,128)S(1)}, f32[2,8,512,2048]{3,2,1,0:T(8,128)}) fusion(f32[2,8,512,2048]{3,2,1,0:T(8,128)} %get-tuple-element.85, f32[2,8,512]{2,1,0:T(8,128)S(1)} %get-tuple-element.84, bf16[2,512,8,64]{1,3,2,0:T(8,128)(2,1)S(1)} %copy-done.27, bf16[2,2048,16,64]{1,3,2,0:T(8,128)(2,1)} %bitcast.163), kind=kOutput, calls=%fused_computation.3 | convolution fusion | flops 2197807104 | bytes 139526144 | tf_op jit(solution)/shard_map/sqhe,skhe->shqk/dot_general | solution.py:211
  662.8 53.4 %multiply_convert_fusion = bf16[2,8,512,2048]{3,2,1,0:T(8,128)(2,1)} fusion(f32[2,8,512,2048]{3,2,1,0:T(8,128)} %get-tuple-element.89, f32[2,8,512]{2,1,0:T(8,128)S(1)} %get-tuple-element.88, f32[2,8,512,2048]{3,2,1,0:T(8,128)} %get-tuple-element.85, f32[2,8,512]{2,1,0:T(8,128)S(1)} %get-tuple-element.84), kind=kLoop, calls=%fused_computation.2 | loop fusion | flops 67108864 | bytes 167837696 | tf_op jit(solution)/shard_map/convert_element_type | solution.py:215
  716.2 17.6 multiply_bitcast_fusion
  733.8 44.9 %multiply_reduce_fusion.1 = (f32[2,8,512]{2,1,0:T(8,128)S(1)}, f32[2,8,512,2048]{3,2,1,0:T(8,128)}) fusion(f32[2,8,512,2048]{3,2,1,0:T(8,128)} %get-tuple-element.87, f32[2,8,512]{2,1,0:T(8,128)S(1)} %copy-done.52, bf16[2,512,8,64]{1,3,2,0:T(8,128)(2,1)S(1)} %copy-done.26, bf16[2,2048,16,64]{1,3,2,0:T(8,128)(2,1)} %bitcast.164), kind=kOutput, calls=%fused_computation.5 | convolution fusion | flops 2197807104 | bytes 139526144 | tf_op jit(solution)/shard_map/sqhe,skhe->shqk/dot_general | solution.py:211
  778.7 53.6 %multiply_convert_fusion.1 = bf16[2,8,512,2048]{3,2,1,0:T(8,128)(2,1)} fusion(f32[2,8,512,2048]{3,2,1,0:T(8,128)} %get-tuple-element.91, f32[2,8,512]{2,1,0:T(8,128)S(1)} %get-tuple-element.90, f32[2,8,512,2048]{3,2,1,0:T(8,128)} %get-tuple-element.87, f32[2,8,512]{2,1,0:T(8,128)S(1)} %copy-done.52), kind=kLoop, calls=%fused_computation.4 | loop fusion | flops 67108864 | bytes 167837696 | tf_op jit(solution)/shard_map/convert_element_type | solution.py:215
  832.2 17.9 multiply_bitcast_fusion.1
  850.1 11.9 pad_maximum_fusion
  863.7 14.9 fusion.103
  878.6 25.2 %fusion.67 = bf16[2,512,8,64]{1,3,2,0:T(8,128)(2,1)S(1)} fusion(bf16[2,2048,16,64]{1,3,2,0:T(8,128)(2,1)} %bitcast.165, f32[2,8,512,2048]{3,2,1,0:T(8,128)} %get-tuple-element.85, f32[2,8,512]{2,1,0:T(8,128)S(1)} %copy-done.50), kind=kOutput, calls=%fused_computation.124 | convolution fusion | flops 2181038080 | bytes 76578816 | tf_op jit(solution)/shard_map/shqk,skhe->sqhe/dot_general | solution.py:162
  903.8 25.6 %fusion.64 = bf16[2,512,8,64]{1,3,2,0:T(8,128)(2,1)} fusion(bf16[2,2048,16,64]{1,3,2,0:T(8,128)(2,1)} %bitcast.166, f32[2,8,512,2048]{3,2,1,0:T(8,128)} %get-tuple-element.87, f32[2,8,512]{2,1,0:T(8,128)S(1)} %copy-done.53), kind=kOutput, calls=%fused_computation.123 | convolution fusion | flops 2181038080 | bytes 76578816 | tf_op jit(solution)/shard_map/shqk,skhe->sqhe/dot_general | solution.py:162
  935.0 4.4 fusion.105
  939.4 51.8 %convert_reduce_fusion = (f32[4096]{0:T(1024)}, bf16[1024,4096]{1,0:T(8,128)(2,1)S(1)}, f32[1024,4096]{1,0:T(8,128)}) fusion(f32[1024,4096]{1,0:T(8,128)} %fusion.103, f32[4096]{0:T(1024)S(1)} %bitcast.188, bf16[1024,1024]{1,0:T(8,128)(2,1)S(1)} %bitcast.180, bf16[4096,1024]{1,0:T(8,128)(2,1)} %all-gather.17.cloned.1.call-done), kind=kOutput, calls=%fused_computation.24 | convolution fusion | flops 8904503296 | bytes 52461568 | tf_op jit(solution)/shard_map/dot_general | solution.py:192
  994.6 11.5 fusion.106
  1006.2 12.2 multiply_convert_fusion.2
  1021.9 11.5 fusion.107
  1033.5 19.1 multiply_bitcast_fusion.2
  1052.6 18.5 multiply_bitcast_fusion.3
  1077.2 3.9 copy.66
  1081.2 172.5 %reduce-scatter.8.cloned.1.call-done = f32[2,512,1024]{1,2,0:T(8,128)} async-done(((f32[2,2048,1024]{1,2,0:T(8,128)}), f32[2,512,1024]{1,2,0:T(8,128)}) %reduce-scatter.8.cloned.1.call-update) | async-done | bytes 4194320 | tf_op jit(solution)/shard_map/reduce_scatter | solution.py:238
  1267.3 13.8 fusion.83
  1283.1 15.5 fusion.104
  1298.7 4.6 convert_reduce_fusion.1
  1303.3 14.2 fusion.88
  1317.5 5.3 fusion.55
  1324.4 178.5 %reduce-scatter.16.cloned.1.call-done = f32[1024,2048]{1,0:T(8,128)} async-done(((f32[1024,4096]{1,0:T(8,128)}), f32[1024,2048]{1,0:T(8,128)}) %reduce-scatter.16.cloned.1.call-update) | async-done | bytes 8388624 | tf_op jit(solution)/shard_map/reduce_scatter | solution.py:280
  1503.0 191.5 %reduce-scatter.18.cloned.1.call-done = f32[4096,512]{1,0:T(8,128)} async-done(((f32[4096,1024]{1,0:T(8,128)}), f32[4096,512]{1,0:T(8,128)}) %reduce-scatter.18.cloned.1.call-update) | async-done | bytes 8388624 | tf_op jit(solution)/shard_map/reduce_scatter | solution.py:281
  1694.4 146.8 %reduce-scatter.12.cloned.1.call-done = f32[1024,1536]{1,0:T(8,128)} async-done(((f32[1024,3072]{1,0:T(8,128)}), f32[1024,1536]{1,0:T(8,128)}) %reduce-scatter.12.cloned.1.call-update) | async-done | bytes 6291472 | tf_op jit(solution)/shard_map/reduce_scatter | solution.py:278
  1841.3 4.6 fusion.102
  1845.9 14.9 fusion.61
  1860.9 4.4 add_add_fusion.2
  1865.4 66.4 %psum.39 = f32[13,512]{1,0:T(8,128)S(1)} all-reduce(f32[13,512]{1,0:T(8,128)} %reduce-scatter.20.cloned.1.call-done), channel_id=1, replica_groups=mesh['batch'=4,'group'=2,'ctx'=4] {'batch','ctx'}, use_global_device_ids=true, to_apply=%region_30.31 | all-reduce | flops 6656 | bytes 53248 | tf_op jit(solution)/shard_map/psum | solution.py:284
  1932.4 372.4 %all-reduce.11.cloned.1.call-done = (f32[1024,1536]{1,0:T(8,128)}, f32[1024,512]{1,0:T(8,128)}, f32[1024,2048]{1,0:T(8,128)}, f32[4096,512]{1,0:T(8,128)}) async-done(((f32[1024,1536]{1,0:T(8,128)}, f32[1024,512]{1,0:T(8,128)}, f32[1024,2048]{1,0:T(8,128)}, f32[4096,512]{1,0:T(8,128)}), (f32[1024,1536]{1,0:T(8,128)}, f32[1024,512]{1,0:T(8,128)}, f32[1024,2048]{1,0:T(8,128)}, ...) | async-done | bytes 25165840 | tf_op jit(solution)/shard_map/psum | solution.py:284
  2304.8 7.5 multiply_subtract_fusion.3
  2312.3 13.1 multiply_subtract_fusion.2
  2325.4 22.2 multiply_subtract_fusion.1
  2347.7 22.4 multiply_subtract_fusion
  (224 shorter events, 82.3 us)
Async XLA Ops:
  7.2 7.9 copy-start.36
  7.2 14.5 copy-start
  7.2 88.3 %all-gather.7.cloned.1.call-start = ((), (), s32[]{:S(2)}) async-start(), calls=%async_computation.7 | async-start | bytes 9437184 | tf_op jit(solution)/shard_map/all_gather | solution.py:103
  12.3 185.9 %all-gather.13.cloned.1.call-start = ((), (), s32[]{:S(2)}) async-start(), calls=%async_computation.10 | async-start | bytes 3145728 | tf_op jit(solution)/shard_map/all_gather | solution.py:104
  15.0 312.3 %all-gather.11.cloned.1.call-start = ((), (), s32[]{:S(2)}) async-start(), calls=%async_computation.9 | async-start | bytes 10485760 | tf_op jit(solution)/shard_map/all_gather | solution.py:141
  21.6 83.3 %copy-start.39 = (f32[1,1024]{1,0:T(1,128)}, f32[1,1024]{1,0:T(1,128)S(1)}, u32[]{:S(2)}) copy-start(f32[1,1024]{1,0:T(1,128)S(1)} %get-tuple-element.72) | copy-start | bytes 12292
  21.6 83.3 %copy-start.41 = (f32[1,1024]{1,0:T(1,128)}, f32[1,1024]{1,0:T(1,128)S(1)}, u32[]{:S(2)}) copy-start(f32[1,1024]{1,0:T(1,128)S(1)} %get-tuple-element.76) | copy-start | bytes 12292
  22.0 82.9 %copy-start.43 = (f32[1,4,2,128]{3,1,2,0:T(4,128)}, f32[1,4,2,128]{3,1,2,0:T(4,128)S(1)}, u32[]{:S(2)}) copy-start(f32[1,4,2,128]{3,1,2,0:T(4,128)S(1)} %copy.80) | copy-start | bytes 12292
  23.4 81.6 %copy-start.45 = (f32[1024]{0:T(1024)}, f32[1024]{0:T(1024)S(1)}, u32[]{:S(2)}) copy-start(f32[1024]{0:T(1024)S(1)} %rsqrt.13) | copy-start | bytes 12292
  23.5 145.6 %copy-start.32 = (f32[512,16]{0,1:T(8,128)}, f32[512,16]{0,1:T(8,128)S(1)}, u32[]{:S(2)}) copy-start(f32[512,16]{0,1:T(8,128)S(1)} %get-tuple-element.78) | copy-start | bytes 98308
  23.5 145.6 %copy-start.34 = (f32[512,16]{0,1:T(8,128)}, f32[512,16]{0,1:T(8,128)S(1)}, u32[]{:S(2)}) copy-start(f32[512,16]{0,1:T(8,128)S(1)} %get-tuple-element.79) | copy-start | bytes 98308
  104.9 7.1 copy-start.5
  156.8 12.3 slice-start.2
  162.8 6.1 copy-start.22
  177.2 429.5 %all-gather.9.cloned.1.call-start = ((), (), s32[]{:S(2)}) async-start(), calls=%async_computation.8 | async-start | bytes 10485760 | tf_op jit(solution)/shard_map/all_gather | solution.py:142
  181.1 682.3 %all-gather.15.cloned.1.call-start = ((), (), s32[]{:S(2)}) async-start(), calls=%async_computation.11 | async-start | bytes 12582912 | tf_op jit(solution)/shard_map/all_gather | solution.py:105
  187.5 7.5 copy-start.56
  187.5 10.6 copy-start.13
  187.5 751.9 %all-gather.17.cloned.1.call-start = ((), (), s32[]{:S(2)}) async-start(), calls=%async_computation.12 | async-start | bytes 12582912 | tf_op jit(solution)/shard_map/all_gather | solution.py:106
  194.3 879.1 %reduce-scatter.10.cloned.1.call-start = ((), (), s32[]{:S(2)}) async-start(), calls=%async_computation.14 | async-start | bytes 20971520 | tf_op jit(solution)/shard_map/reduce_scatter | solution.py:239
  216.9 110.4 %copy-start.28 = (bf16[2,512,16,16]{1,3,2,0:T(8,128)(2,1)S(1)}, bf16[2,512,16,16]{1,3,2,0:T(8,128)(2,1)}, u32[]{:S(2)}) copy-start(bf16[2,512,16,16]{1,3,2,0:T(8,128)(2,1)} %get-tuple-element.67) | copy-start | bytes 1572868
  230.2 97.1 %copy-start.23 = (bf16[2,512,16,48]{1,3,2,0:T(8,128)(2,1)}, bf16[2,512,16,48]{1,3,2,0:T(8,128)(2,1)S(1)}, u32[]{:S(2)}) copy-start(bf16[2,512,16,48]{1,3,2,0:T(8,128)(2,1)S(1)} %copy.79) | copy-start | bytes 4718596
  354.9 25.8 %copy-start.17 = (pred[2,512,2048]{2,1,0:T(8,128)(4,1)S(1)}, pred[2,512,2048]{2,1,0:T(8,128)(4,1)}, u32[]{:S(2)}) copy-start(pred[2,512,2048]{2,1,0:T(8,128)(4,1)} %compare_and_fusion) | copy-start | bytes 6291460
  449.9 212.8 %copy-start.49 = (f32[2,8,512]{2,1,0:T(8,128)}, f32[2,8,512]{2,1,0:T(8,128)S(1)}, u32[]{:S(2)}) copy-start(f32[2,8,512]{2,1,0:T(8,128)S(1)} %get-tuple-element.84) | copy-start | bytes 98308
  449.9 74.3 %copy-start.27 = (bf16[2,512,8,64]{1,3,2,0:T(8,128)(2,1)S(1)}, bf16[2,512,8,64]{1,3,2,0:T(8,128)(2,1)}, u32[]{:S(2)}) copy-start(bf16[2,512,8,64]{1,3,2,0:T(8,128)(2,1)} %copy.75) | copy-start | bytes 3145732
  524.3 25.9 %copy-start.51 = (f32[2,8,512]{2,1,0:T(8,128)}, f32[2,8,512]{2,1,0:T(8,128)S(1)}, u32[]{:S(2)}) copy-start(f32[2,8,512]{2,1,0:T(8,128)S(1)} %get-tuple-element.86) | copy-start | bytes 98308
  524.3 25.9 %copy-start.25 = (bf16[2,512,8,64]{1,3,2,0:T(8,128)(2,1)S(1)}, bf16[2,512,8,64]{1,3,2,0:T(8,128)(2,1)}, u32[]{:S(2)}) copy-start(bf16[2,512,8,64]{1,3,2,0:T(8,128)(2,1)} %copy.74) | copy-start | bytes 3145732
  662.7 590.9 %reduce-scatter.8.cloned.1.call-start = ((), (), s32[]{:S(2)}) async-start(), calls=%async_computation.13 | async-start | bytes 20971520 | tf_op jit(solution)/shard_map/reduce_scatter | solution.py:238
  662.7 53.5 %copy-start.24 = (bf16[2,512,16,48]{1,3,2,0:T(8,128)(2,1)S(1)}, bf16[2,512,16,48]{1,3,2,0:T(8,128)(2,1)}, u32[]{:S(2)}) copy-start(bf16[2,512,16,48]{1,3,2,0:T(8,128)(2,1)} %copy-done.23) | copy-start | bytes 4718596
  662.7 53.5 %copy-start.29 = (bf16[2,512,16,16]{1,3,2,0:T(8,128)(2,1)S(1)}, bf16[2,512,16,16]{1,3,2,0:T(8,128)(2,1)}, u32[]{:S(2)}) copy-start(bf16[2,512,16,16]{1,3,2,0:T(8,128)(2,1)} %get-tuple-element.67) | copy-start | bytes 1572868
  716.2 17.6 copy-start.26
  716.2 17.6 copy-start.52
  862.1 462.3 %reduce-scatter.14.cloned.1.call-start = ((), (), s32[]{:S(2)}) async-start(), calls=%async_computation.16 | async-start | bytes 6291456 | tf_op jit(solution)/shard_map/reduce_scatter | solution.py:279
  863.7 14.9 copy-start.50
  878.6 25.2 %copy-start.53 = (f32[2,8,512]{2,1,0:T(8,128)S(1)}, f32[2,8,512]{2,1,0:T(8,128)}, u32[]{:S(2)}) copy-start(f32[2,8,512]{2,1,0:T(8,128)} %copy-done.51) | copy-start | bytes 98308
  929.3 5.6 copy-start.14
  935.0 4.5 copy-start.38
  939.3 563.6 %reduce-scatter.16.cloned.1.call-start = ((), (), s32[]{:S(2)}) async-start(), calls=%async_computation.17 | async-start | bytes 25165824 | tf_op jit(solution)/shard_map/reduce_scatter | solution.py:280
  939.4 55.2 %copy-start.20 = (bf16[1024,1024]{1,0:T(8,128)(2,1)S(1)}, bf16[1024,1024]{1,0:T(8,128)(2,1)}, u32[]{:S(2)}) copy-start(bf16[1024,1024]{1,0:T(8,128)(2,1)} %get-tuple-element.59) | copy-start | bytes 6291460
  1006.2 688.3 %reduce-scatter.18.cloned.1.call-start = ((), (), s32[]{:S(2)}) async-start(), calls=%async_computation.18 | async-start | bytes 25165824 | tf_op jit(solution)/shard_map/reduce_scatter | solution.py:281
  1033.4 807.8 %reduce-scatter.12.cloned.1.call-start = ((), (), s32[]{:S(2)}) async-start(), calls=%async_computation.15 | async-start | bytes 18874368 | tf_op jit(solution)/shard_map/reduce_scatter | solution.py:278
  1073.3 182.5 %copy-start.35 = (f32[512,16]{0,1:T(8,128)S(1)}, f32[512,16]{0,1:T(8,128)}, u32[]{:S(2)}) copy-start(f32[512,16]{0,1:T(8,128)} %copy-done.34) | copy-start | bytes 98308
  1281.1 584.3 %reduce-scatter.20.cloned.1.call-start = ((), (), s32[]{:S(2)}) async-start(), calls=%async_computation.19 | async-start | bytes 98304 | tf_op jit(solution)/shard_map/reduce_scatter | solution.py:282
  1283.0 15.6 copy-start.8
  1283.0 15.6 copy-start.10
  1283.1 15.6 copy-start.12
  1283.1 20.2 copy-start.1
  1283.1 20.2 copy-start.40
  1283.1 20.2 copy-start.42
  1283.1 20.2 copy-start.44
  1303.3 14.2 copy-start.48
  1303.3 14.2 copy-start.2
  1303.3 14.2 copy-start.46
  1324.1 980.7 %all-reduce.11.cloned.1.call-start = ((), (), s32[]{:S(2)}) async-start(), calls=%async_computation.20 | async-start | bytes 50331648 | tf_op jit(solution)/shard_map/psum | solution.py:284
  1841.2 4.6 copy-start.58
  1841.2 4.6 copy-start.59
  1845.9 15.0 copy-start.3
  1845.9 15.0 copy-start.4
  1845.9 15.0 copy-start.16
  1860.9 70.9 %copy-start.37 = (f32[13,512]{1,0:T(8,128)S(1)}, f32[13,512]{1,0:T(8,128)}, u32[]{:S(2)}) copy-start(f32[13,512]{1,0:T(8,128)} %param.33) | copy-start | bytes 79876
  1860.9 70.9 %copy-start.54 = (f32[13,512]{1,0:T(8,128)S(1)}, f32[13,512]{1,0:T(8,128)}, u32[]{:S(2)}) copy-start(f32[13,512]{1,0:T(8,128)} %param.34) | copy-start | bytes 79876
  1860.9 70.9 %copy-start.55 = (f32[13,512]{1,0:T(8,128)S(1)}, f32[13,512]{1,0:T(8,128)}, u32[]{:S(2)}) copy-start(f32[13,512]{1,0:T(8,128)} %param.35) | copy-start | bytes 79876
  1865.4 447.0 %slice-start = ((s8[6291456]{0:T(1024)(128)(4,1)}), s8[2097152]{0:T(1024)(128)(4,1)S(1)}, s32[]{:S(2)}) async-start(s8[6291456]{0:T(1024)(128)(4,1)} %bitcast.160), calls=%async_computation.21 | async-start | bytes 4194304
  2304.8 7.5 slice-start.1
  (14 other events, 33.0 us)
Sparse Core Ops, SparseCore 0:
  12.4 83.0 all-gather.6
  97.6 33.1 all-gather.12
  177.3 149.9 all-gather.10
  329.3 147.8 all-gather.8
  479.2 102.1 all-gather.14
  583.3 103.9 all-gather.16
  689.7 280.3 reduce-scatter.9
  972.6 280.9 reduce-scatter.7
  1256.5 55.0 reduce-scatter.13
  1313.8 189.1 reduce-scatter.15
  1505.3 189.1 reduce-scatter.17
  1696.7 144.4 reduce-scatter.11
  1844.0 9.8 reduce-scatter.19
  1859.4 445.3 all-reduce.10
where the time goes:
time: 2390 us; the launch traced here: 2380 us
  waiting for transfers between devices  1230 us (51%)
  matrix products  490 us (21%)
  other arithmetic  414 us (17%)
  local copies, waits for them, and re-layouts  157 us (7%)
  blocking collectives  71.7 us (3%)
    psum x1, waiting for transfers between devices, local(): lax.psum((owned_part[0], owned_part[1], owned_part[2], owned_part[3], own...  372 us
    reduce_scatter x1, waiting for transfers between devices, local(): lax.psum_scatter(shrink_grad, 'group', scatter_dimension=1, tiled=True)  191 us
    reduce_scatter x1, waiting for transfers between devices, local(): lax.psum_scatter(expand_grad, 'group', scatter_dimension=1, tiled=True)  179 us
    reduce_scatter x1, waiting for transfers between devices, local(): lax.psum_scatter(key_grad_all, 'ctx', scatter_dimension=1, tiled=True)  172 us
    reduce_scatter x1, waiting for transfers between devices, local(): lax.psum_scatter(inward_grad, 'group', scatter_dimension=1, tiled=True)  147 us
    sub x2, other arithmetic, local(): lifted = jnp.exp(scores - row_top)  144 us
    convert_element_type x2, other arithmetic, local(): score_grad = (attn_probs * (prob_grad - row_weight)).astype(jnp.bfloat16)  107 us
    all_gather x1, waiting for transfers between devices, local(): lax.all_gather(key_low, 'ctx', axis=1, tiled=True)  97.1 us
  transfers between devices with their start and end apart: 14, of which 7 were waited for; matrix products, arithmetic and copies ran while one was open for 41% of the time, Pallas kernels for 0%

commit v1 on v0

v1 whole, which is shorter than its diff:
```python
import functools
import math

import jax
import jax.numpy as jnp
from jax import lax
from jax.experimental import pallas as pl
from jax.experimental.pallas import tpu as pltpu
from jax.sharding import PartitionSpec as P

HEADS = 16
ROTARY = 16
STEP = 10


norm_eps = 1e-05
adam_eps = 1e-08
first_decay = 0.9
second_decay = 0.95
decay_rate = 0.01
matrix_rate = 0.1
vector_rate = 0.8
neg_fill = -1e30


def layer_norm(values, norm_gain, norm_shift):
    row_mean = jnp.mean(values, -1, keepdims=True)
    centred = values - row_mean
    variance = jnp.mean(centred * centred, -1, keepdims=True)
    return centred * lax.rsqrt(variance + norm_eps) * norm_gain + norm_shift


def lane_tables(positions, head_size, width):
    half_rot = ROTARY // 2
    lane = jnp.arange(width) % head_size
    frequency = jnp.exp(
        (lane % half_rot).astype(jnp.float32) * (-2.0 * math.log(10000.0) / ROTARY)
    )
    angles = positions[:, None] * frequency[None, :]
    cosine = jnp.where(lane < ROTARY, jnp.cos(angles), 1.0)
    sine = jnp.where(lane < ROTARY, jnp.sin(angles), 0.0)
    return cosine, jnp.where(lane < half_rot, -sine, sine)


def spin(values, cosine, signed_sine):
    half_rot = ROTARY // 2
    width = values.shape[-1]
    lane = lax.broadcasted_iota(jnp.int32, values.shape, 1) % 64
    partner = jnp.where(
        lane < half_rot,
        pltpu.roll(values, width - half_rot, 1),
        pltpu.roll(values, half_rot, 1),
    )
    return values * cosine + partner * signed_sine


def joint_kernel(score_scale, q_blocks, rows_ref, weight_ref, bias_ref, cos_ref, sin_ref, q_ref, kv_ref):
    place = pl.program_id(0)
    tok_count = cos_ref.shape[0]
    seq_count = rows_ref.shape[0] // tok_count
    width = weight_ref.shape[1]
    for seq in range(seq_count):
        span = pl.ds(seq * tok_count, tok_count)
        product = (
            jnp.dot(rows_ref[span, :], weight_ref[...], preferred_element_type=jnp.float32)
            + bias_ref[...]
        )

        @pl.when(place < 2 * q_blocks)
        def _():
            for first in range(0, width, 128):
                turned = spin(product[:, first : first + 128], cos_ref[...], sin_ref[...])

                @pl.when(place < q_blocks)
                def _():
                    low = turned.astype(jnp.bfloat16).astype(jnp.float32) * score_scale
                    q_ref[span, first : first + 128] = low.astype(jnp.bfloat16)

                @pl.when(place >= q_blocks)
                def _():
                    kv_ref[span, first : first + 128] = turned.astype(jnp.bfloat16)

        @pl.when(place >= 2 * q_blocks)
        def _():
            kv_ref[span, :] = product.astype(jnp.bfloat16)


def project_joint(rows, weight, bias, cosine, sine, score_scale):
    row_count, width = rows.shape
    block = 512
    q_blocks = width // block
    whole = lambda j: (0, 0)
    return pl.pallas_call(
        functools.partial(joint_kernel, score_scale, q_blocks),
        grid=(3 * q_blocks,),
        in_specs=[
            pl.BlockSpec((row_count, width), whole),
            pl.BlockSpec((width, block), lambda j: (0, j)),
            pl.BlockSpec((1, block), lambda j: (0, j)),
            pl.BlockSpec(cosine.shape, whole),
            pl.BlockSpec(sine.shape, whole),
        ],
        out_specs=[
            pl.BlockSpec((row_count, block), lambda j: (0, jnp.minimum(j, q_blocks - 1))),
            pl.BlockSpec((row_count, block), lambda j: (0, jnp.maximum(j - q_blocks, 0))),
        ],
        out_shape=[
            jax.ShapeDtypeStruct((row_count, width), jnp.bfloat16),
            jax.ShapeDtypeStruct((row_count, 2 * width), jnp.bfloat16),
        ],
        compiler_params=pltpu.CompilerParams(vmem_limit_bytes=40 * 2**20),
        cost_estimate=pl.CostEstimate(
            flops=6 * row_count * width * width, bytes_accessed=14 * 2**20, transcendentals=0
        ),
        name="joint_projection",
    )(rows, weight, bias, cosine, sine)


def attend_kernel(
    chunk, score_scale, q_ref, k_ref, v_ref, g_ref, low_ref, top_ref, cosk_ref, sink_ref,
    cosq_ref, sinq_ref, out_ref, dq_ref, dk_ref, dv_ref, bias_ref, prob_ref, grad_ref,
):
    key_count = k_ref.shape[1]
    tok_count = q_ref.shape[0]
    chunks = key_count // chunk

    @pl.when(pl.program_id(0) == 0)
    def _():
        for c in range(chunks):
            key_place = c * chunk + lax.broadcasted_iota(jnp.int32, (chunk, tok_count), 0)
            kept = (key_place >= low_ref[0]) & (key_place <= top_ref[...])
            bias_ref[c * chunk : (c + 1) * chunk, :] = jnp.where(kept, 0.0, neg_fill)

    nt = (((1,), (1,)), ((), ()))
    tn = (((0,), (0,)), ((), ()))
    lane = lax.broadcasted_iota(jnp.int32, (tok_count, 128), 1)
    head_row = lax.broadcasted_iota(jnp.int32, (128, tok_count), 0)
    spans = [slice(c * chunk, (c + 1) * chunk) for c in range(chunks)]
    outs, dqs = [], []
    for head in range(2):
        own = (lane // 64) == head
        query = jnp.where(own, q_ref[...], jnp.zeros_like(q_ref))
        grad = jnp.where(own, g_ref[...], jnp.zeros_like(g_ref))
        top = None
        for span in spans:
            scores = (
                lax.dot_general(k_ref[0, span, :], query, nt, preferred_element_type=jnp.float32)
                + bias_ref[span, :]
            )
            prob_ref[head, span, :] = scores
            chunk_top = jnp.max(scores, 0, keepdims=True)
            top = chunk_top if top is None else jnp.maximum(top, chunk_top)
        total = jnp.zeros((1, tok_count), jnp.float32)
        weighted = jnp.zeros((1, tok_count), jnp.float32)
        for span in spans:
            lifted = jnp.exp(prob_ref[head, span, :] - top)
            prob_grad = lax.dot_general(
                v_ref[0, span, :], grad, nt, preferred_element_type=jnp.float32
            )
            prob_ref[head, span, :] = lifted
            grad_ref[head, span, :] = prob_grad
            total += jnp.sum(lifted, 0, keepdims=True)
            weighted += jnp.sum(lifted * prob_grad, 0, keepdims=True)
        inverse = 1.0 / total
        weighted = weighted * inverse
        out = jnp.zeros((128, tok_count), jnp.float32)
        dq = jnp.zeros((128, tok_count), jnp.float32)
        for span in spans:
            probs = prob_ref[head, span, :] * inverse
            probs_low = probs.astype(jnp.bfloat16)
            score_grad = (probs * (grad_ref[head, span, :] - weighted)).astype(jnp.bfloat16)
            out += lax.dot_general(v_ref[0, span, :], probs_low, tn, preferred_element_type=jnp.float32)
            dq += lax.dot_general(k_ref[0, span, :], score_grad, tn, preferred_element_type=jnp.float32)
            dv = jnp.dot(probs_low, grad, preferred_element_type=jnp.float32)
            dk = jnp.dot(score_grad, query, preferred_element_type=jnp.float32)
            dk = spin(dk, cosk_ref[span, :], -sink_ref[span, :])
            key_lane = lax.broadcasted_iota(jnp.int32, dk.shape, 1)
            if head == 0:
                dv_ref[span, :] = dv.astype(jnp.bfloat16)
                dk_ref[span, :] = dk.astype(jnp.bfloat16)
            else:
                dv_ref[span, :] = jnp.where(key_lane < 64, dv_ref[span, :], dv.astype(jnp.bfloat16))
                dk_ref[span, :] = jnp.where(key_lane < 64, dk_ref[span, :], dk.astype(jnp.bfloat16))
        outs.append(out)
        dqs.append(dq)
    out_ref[...] = jnp.where(head_row < 64, outs[0], outs[1]).T.astype(jnp.bfloat16)
    dq = jnp.where(head_row < 64, dqs[0], dqs[1]).T * score_scale
    dq_ref[...] = spin(dq, cosq_ref[...], -sinq_ref[...]).astype(jnp.bfloat16)


def attend(seq, query, kv, grad, lows, tops, key_tables, query_tables, score_scale):
    tok_count = tops.shape[1]
    width = query.shape[1]
    key_count = kv.shape[1]
    pairs = width // 128
    whole = lambda j: (0, 0)
    columns = lambda j: (0, j)
    own = lambda j: (seq, j)
    return pl.pallas_call(
        functools.partial(attend_kernel, 512, score_scale),
        grid=(pairs,),
        in_specs=[
            pl.BlockSpec((tok_count, 128), own),
            pl.BlockSpec((1, key_count, 128), lambda j: (seq, 0, j)),
            pl.BlockSpec((1, key_count, 128), lambda j: (seq, 0, pairs + j)),
            pl.BlockSpec((tok_count, 128), own),
            pl.BlockSpec((1, 1, tok_count), lambda j: (seq, 0, 0)),
            pl.BlockSpec((1, tok_count), whole),
            pl.BlockSpec((key_count, 128), whole),
            pl.BlockSpec((key_count, 128), whole),
            pl.BlockSpec((tok_count, 128), whole),
            pl.BlockSpec((tok_count, 128), whole),
        ],
        out_specs=[
            pl.BlockSpec((tok_count, 128), columns),
            pl.BlockSpec((tok_count, 128), columns),
            pl.BlockSpec((key_count, 128), columns),
            pl.BlockSpec((key_count, 128), columns),
        ],
        out_shape=[
            jax.ShapeDtypeStruct((tok_count, width), jnp.bfloat16),
            jax.ShapeDtypeStruct((tok_count, width), jnp.bfloat16),
            jax.ShapeDtypeStruct((key_count, width), jnp.bfloat16),
            jax.ShapeDtypeStruct((key_count, width), jnp.bfloat16),
        ],
        scratch_shapes=[
            pltpu.VMEM((key_count, tok_count), jnp.float32),
            pltpu.VMEM((2, key_count, tok_count), jnp.float32),
            pltpu.VMEM((2, key_count, tok_count), jnp.float32),
        ],
        compiler_params=pltpu.CompilerParams(vmem_limit_bytes=56 * 2**20),
        cost_estimate=pl.CostEstimate(
            flops=100 * 10**9, bytes_accessed=20 * 2**20, transcendentals=pairs * 2 * key_count * tok_count
        ),
        name="attention_both_ways",
    )(query, kv, kv, grad, lows, tops, *key_tables, *query_tables)


def gelu_exact(values):
    return jax.nn.gelu(values, approximate=False)


def gather_weight(weight):
    rows = weight.shape[0] // lax.axis_size("ctx")
    part = lax.dynamic_slice_in_dim(weight, lax.axis_index("ctx") * rows, rows, 0)
    part = lax.all_gather(part.astype(jnp.bfloat16), "group", axis=1, tiled=True)
    return lax.all_gather(part, "ctx", axis=0, tiled=True)


def reduce_gradient(gradient):
    part = lax.psum_scatter(gradient, ("ctx", "batch"), scatter_dimension=0, tiled=True)
    part = lax.psum_scatter(part, "group", scatter_dimension=1, tiled=True)
    return lax.all_gather(part, ("ctx", "batch"), axis=0, tiled=True)


def adam_step(weight, moment, square, gradient, rate):
    first = first_decay * moment + (1.0 - first_decay) * gradient
    second = second_decay * square + (1.0 - second_decay) * gradient * gradient
    first_hat = first / (1.0 - first_decay**STEP)
    second_hat = second / (1.0 - second_decay**STEP)
    master = weight - rate * (first_hat / (jnp.sqrt(second_hat) + adam_eps) + decay_rate * weight)
    return (master, first, second)


def update_all(weights, moments, squares, gradients):
    rates = (matrix_rate, matrix_rate, matrix_rate, matrix_rate, vector_rate)
    results = ()
    for place in range(5):
        results = results + adam_step(
            weights[place], moments[place], squares[place], gradients[place], rates[place]
        )
    return results


def local(
    block_input,
    doc_ids,
    out_cotangent,
    inward_weight,
    inward_moment,
    inward_square,
    outward_weight,
    outward_moment,
    outward_square,
    expand_weight,
    expand_moment,
    expand_square,
    shrink_weight,
    shrink_moment,
    shrink_square,
    vector_weight,
    vector_moment,
    vector_square,
):
    vector_full = lax.all_gather(
        vector_weight.astype(jnp.bfloat16), "group", axis=1, tiled=True
    ).astype(jnp.float32)
    inward_copy = gather_weight(inward_weight)
    expand_copy = gather_weight(expand_weight)
    shrink_copy = gather_weight(shrink_weight)
    outward_copy = gather_weight(outward_weight)
    seq_count, tok_count, model_width = block_input.shape
    head_size = model_width // HEADS
    seq_length = doc_ids.shape[1]
    ffn_rows = expand_copy.shape[1] // model_width
    row_count = seq_count * tok_count
    score_scale = head_size ** (-0.5)
    offset = lax.axis_index("ctx") * tok_count
    residual = block_input.astype(jnp.float32).reshape(row_count, model_width)
    normed_attn, attn_norm_back = jax.vjp(layer_norm, residual, vector_full[0], vector_full[1])
    normed_mlp, mlp_norm_back = jax.vjp(layer_norm, residual, vector_full[2], vector_full[3])
    attn_in = normed_attn.astype(jnp.bfloat16)
    mlp_in = normed_mlp.astype(jnp.bfloat16)
    key_tables = lane_tables(jnp.arange(seq_length).astype(jnp.float32), head_size, 128)
    query_places = offset + jnp.arange(tok_count)
    query_tables = lane_tables(query_places.astype(jnp.float32), head_size, 128)
    query_low, kv_low = project_joint(
        attn_in, inward_copy, vector_full[4:7].reshape(1, -1), *query_tables, score_scale
    )
    kv_rows = lax.all_gather(
        kv_low.reshape(seq_count, tok_count, 2 * model_width), "ctx", axis=1, tiled=True
    )
    own_docs = lax.dynamic_slice_in_dim(doc_ids, offset, tok_count, 1)
    cut = jnp.sum((doc_ids == 0).astype(jnp.int32), 1, keepdims=True)
    lows = jnp.where(own_docs == 0, 0, cut)[:, None, :]
    tops = query_places.astype(jnp.int32)[None, :]
    pre_act = jnp.dot(mlp_in, expand_copy, preferred_element_type=jnp.float32) + vector_full[
        8 : 8 + ffn_rows
    ].reshape(-1)
    activation, act_back = jax.vjp(gelu_exact, pre_act)
    act_low = activation.astype(jnp.bfloat16)
    grad_low = out_cotangent.reshape(row_count, model_width)
    grad_out = grad_low.astype(jnp.float32)
    shrink_grad = jnp.dot(act_low.T, grad_low, preferred_element_type=jnp.float32).astype(
        jnp.bfloat16
    )
    act_grad = jnp.dot(grad_low, shrink_copy.T, preferred_element_type=jnp.float32)
    pre_grad = act_back(act_grad)[0].astype(jnp.bfloat16)
    expand_grad = jnp.dot(mlp_in.T, pre_grad, preferred_element_type=jnp.float32).astype(
        jnp.bfloat16
    )
    attended_grad = jnp.dot(grad_low, outward_copy.T, preferred_element_type=jnp.float32).astype(
        jnp.bfloat16
    )
    shrink_grad, expand_grad, attended_grad = lax.optimization_barrier(
        (shrink_grad, expand_grad, attended_grad)
    )
    attended, query_grads, key_grads, value_grads = [], [], [], []
    for seq in range(seq_count):
        out, dq, dk, dv = attend(
            seq, query_low, kv_rows, attended_grad, lows, tops, key_tables, query_tables, score_scale
        )
        attended.append(out)
        query_grads.append(dq)
        key_grads.append(lax.psum_scatter(dk, "ctx", scatter_dimension=0, tiled=True))
        value_grads.append(lax.psum_scatter(dv, "ctx", scatter_dimension=0, tiled=True))
    attn_low = jnp.concatenate(attended, 0)
    outward_grad = jnp.dot(attn_low.T, grad_low, preferred_element_type=jnp.float32).astype(
        jnp.bfloat16
    )
    attn_out = jnp.dot(attn_low, outward_copy, preferred_element_type=jnp.float32) + vector_full[7]
    mlp_out = (
        jnp.dot(act_low, shrink_copy, preferred_element_type=jnp.float32)
        + vector_full[8 + ffn_rows]
    )
    block_output = (
        (residual + attn_out + mlp_out)
        .astype(jnp.bfloat16)
        .reshape(seq_count, tok_count, model_width)
    )
    mlp_in_grad = jnp.dot(pre_grad, expand_copy.T, preferred_element_type=jnp.float32)
    joint_grad = jnp.concatenate(
        [
            jnp.concatenate(query_grads, 0),
            jnp.concatenate(key_grads, 0),
            jnp.concatenate(value_grads, 0),
        ],
        -1,
    )
    inward_grad = jnp.dot(attn_in.T, joint_grad, preferred_element_type=jnp.float32).astype(
        jnp.bfloat16
    )
    attn_in_grad = jnp.dot(joint_grad, inward_copy.T, preferred_element_type=jnp.float32)
    residual_attn, gain_attn, shift_attn = attn_norm_back(attn_in_grad)
    residual_mlp, gain_mlp, shift_mlp = mlp_norm_back(mlp_in_grad)
    input_grad = (grad_out + residual_attn + residual_mlp).reshape(
        seq_count, tok_count, model_width
    )
    joint_sum = jnp.sum(joint_grad.astype(jnp.float32), 0).reshape(3, model_width)
    out_sum = jnp.sum(grad_out, 0)
    pre_sum = jnp.sum(pre_grad.astype(jnp.float32), 0).reshape(ffn_rows, model_width)
    vector_grad = jnp.concatenate(
        [
            gain_attn[None],
            shift_attn[None],
            gain_mlp[None],
            shift_mlp[None],
            joint_sum,
            out_sum[None],
            pre_sum,
            out_sum[None],
        ],
        0,
    )
    vector_sum = lax.psum(vector_grad, ("batch", "group", "ctx"))
    own_width = vector_weight.shape[1]
    vector_own = lax.dynamic_slice_in_dim(
        vector_sum, lax.axis_index("group") * own_width, own_width, 1
    )
    masters = (inward_weight, outward_weight, expand_weight, shrink_weight, vector_weight)
    moments = (inward_moment, outward_moment, expand_moment, shrink_moment, vector_moment)
    squares = (inward_square, outward_square, expand_square, shrink_square, vector_square)
    summed = tuple(
        reduce_gradient(gradient).astype(jnp.float32)
        for gradient in (inward_grad, outward_grad, expand_grad, shrink_grad)
    ) + (vector_own,)
    results = update_all(masters, moments, squares, summed)
    return (block_output, input_grad) + tuple(results)


def solution(mesh):
    placed = (
        P(("batch", "group"), "ctx", None),
        P(("batch", "group"), None),
        P(("batch", "group"), "ctx", None),
        P(None, "group"),
        P(None, "group"),
        P(None, "group"),
        P(None, "group"),
        P(None, "group"),
        P(None, "group"),
        P(None, "group"),
        P(None, "group"),
        P(None, "group"),
        P(None, "group"),
        P(None, "group"),
        P(None, "group"),
        P(None, "group"),
        P(None, "group"),
        P(None, "group"),
    )
    return jax.shard_map(
        local,
        mesh=mesh,
        in_specs=placed,
        out_specs=(
            P(("batch", "group"), "ctx", None),
            P(("batch", "group"), "ctx", None),
            P(None, "group"),
            P(None, "group"),
            P(None, "group"),
            P(None, "group"),
            P(None, "group"),
            P(None, "group"),
            P(None, "group"),
            P(None, "group"),
            P(None, "group"),
            P(None, "group"),
            P(None, "group"),
            P(None, "group"),
            P(None, "group"),
            P(None, "group"),
            P(None, "group"),
        ),
        check_vma=False,
    )
```

time: 2390 us -> 1850 us (0.77)
  matrix products: 490 us -> 170 us
  other arithmetic: 414 us -> 99.2 us
  Pallas kernels: 0 us -> 164 us
  local copies, waits for them, and re-layouts: 157 us -> 20 us
  waiting for transfers between devices: 1230 us -> 1330 us
    all_gather x6 -> x12, waiting for transfers between devices: 166 us -> 779 us  [the longest x4 374 us: gather_weight(): return lax.all_gather(part, 'ctx', axis=0, tiled=True)]
    psum x1 -> x0, waiting for transfers between devices: 372 us -> none  [local(): lax.psum((owned_part[0], owned_part[1], owned_part[2], owned_part[3], own...]
    dot_general x13 -> x0, matrix products: 327 us -> none  [the longest x2 89.2 us: local(): jnp.einsum('sqhe,skhe->shqk', grad_part, value_part, preferred_element_ty...]
    pallas_call x0 -> x3, Pallas kernels: none -> 164 us  [the longest x2 146 us: attend(): pl.pallas_call(functools.partial(attend_kernel, 512, score_scale), grid=(...]
    reduce_scatter x7 -> x12, waiting for transfers between devices: 689 us -> 543 us  [the longest x4 241 us: reduce_gradient(): lax.psum_scatter(gradient, ('ctx', 'batch'), scatter_dimension=0, tiled=T...]
    sub x2 -> x0, other arithmetic: 144 us -> none  [local(): lifted = jnp.exp(scores - row_top)]
    convert_element_type x9 -> x3, other arithmetic: 141 us -> 0.02 us  [the longest x1 0.01 us: local(): vector_full = lax.all_gather(vector_weight.astype(jnp.bfloat16), 'group',...]
    reshape x5 -> x0, local copies, waits for them, and re-layouts: 43 us -> none  [the longest x1 18.9 us: local(): jnp.concatenate(value_grads, 2).reshape(seq_count, seq_length, model_width)]
  transfers between devices with their start and end apart: 14 -> 24, of which waited for: 7 -> 20; matrix products, arithmetic and copies ran while one was open for 41% -> 14% of each run, Pallas kernels for 0% -> 9%
where the time goes in v1:
time: 1850 us
  waiting for transfers between devices  1330 us (72%)
  matrix products  170 us (9%)
  Pallas kernels  164 us (9%)
  other arithmetic  99.2 us (5%)
  blocking collectives  52.8 us (3%)
  local copies, waits for them, and re-layouts  20 us (1%)
    all_gather x4, waiting for transfers between devices, gather_weight(): return lax.all_gather(part, 'ctx', axis=0, tiled=True)  374 us
    reduce_scatter x4, waiting for transfers between devices, reduce_gradient(): lax.psum_scatter(gradient, ('ctx', 'batch'), scatter_dimension=0, tiled=T...  241 us
    all_gather x1, waiting for transfers between devices, local(): lax.all_gather(kv_low.reshape(seq_count, tok_count, 2 * model_width), 'ct...  223 us
    reduce_scatter x2, waiting for transfers between devices, local(): lax.psum_scatter(dv, 'ctx', scatter_dimension=0, tiled=True)  161 us
    pallas_call x2, Pallas kernels, attend(): pl.pallas_call(functools.partial(attend_kernel, 512, score_scale), grid=(...  146 us
    reduce_scatter x2, waiting for transfers between devices, local(): lax.psum_scatter(dk, 'ctx', scatter_dimension=0, tiled=True)  110 us
    all_gather x4, waiting for transfers between devices, reduce_gradient(): return lax.all_gather(part, ('ctx', 'batch'), axis=0, tiled=True)  96.2 us
    all_gather x3, waiting for transfers between devices, gather_weight(): lax.all_gather(part.astype(jnp.bfloat16), 'group', axis=1, tiled=True)  85.1 us
  transfers between devices with their start and end apart: 24, of which 20 were waited for; matrix products, arithmetic and copies ran while one was open for 14% of the time, Pallas kernels for 9%

profile of v1, /device:TPU:0, one launch (start us, length us, event | category | flops | bytes accessed | tf_op | source)
XLA Modules:
  0.0 1847.7 jit_solution(7879334930441912236)
XLA Ops:
  7.2 2.4 dynamic-slice_convert_fusion.2
  9.7 2.7 dynamic-slice_convert_fusion.1
  12.5 2.8 dynamic-slice_convert_fusion
  15.4 24.7 %all-gather.13.cloned.1.call-done = bf16[256,3072]{1,0:T(8,128)(2,1)} async-done(((bf16[256,1536]{1,0:T(8,128)(2,1)}), bf16[256,3072]{1,0:T(8,128)(2,1)}) %all-gather.13.cloned.1.call-update) | async-done | bytes 1572880 | tf_op jit(solution)/shard_map/all_gather | solution.py:246
  40.1 1.1 dynamic-slice_convert_fusion.3
  41.2 8.8 all_gather.50
  50.1 25.2 %all-gather.19.cloned.1.call-done = bf16[256,4096]{1,0:T(8,128)(2,1)} async-done(((bf16[256,2048]{1,0:T(8,128)(2,1)}), bf16[256,4096]{1,0:T(8,128)(2,1)}) %all-gather.19.cloned.1.call-update) | async-done | bytes 2097168 | tf_op jit(solution)/shard_map/all_gather | solution.py:246
  75.4 35.2 %all-gather.23.cloned.1.call-done = bf16[1024,1024]{1,0:T(8,128)(2,1)} async-done(((bf16[1024,512]{1,0:T(8,128)(2,1)}), bf16[1024,1024]{1,0:T(8,128)(2,1)}) %all-gather.23.cloned.1.call-update) | async-done | bytes 2097168 | tf_op jit(solution)/shard_map/all_gather | solution.py:246
  111.1 0.7 fusion.37
  111.9 4.4 all_gather.42
  116.4 0.6 fusion.67
  117.0 1.0 negate_select_fusion.1
  118.1 3.8 fusion.31
  121.9 105.5 %all-gather.15.cloned.1.call-done.weight_ref = bf16[1024,3072]{1,0:T(8,128)(2,1)} async-done(((bf16[256,3072]{1,0:T(8,128)(2,1)}), bf16[1024,3072]{1,0:T(8,128)(2,1)}) %all-gather.15.cloned.1.call-update) | async-done | bytes 6291472 | tf_op jit(solution)/shard_map/all_gather | solution.py:247
  227.4 18.1 joint_projection.1
  245.6 2.0 copy-done
  247.6 1.3 copy-done.3
  249.2 24.1 %all-gather.27.cloned.1.call-done = bf16[1024,1024]{1,0:T(8,128)(2,1)} async-done(((bf16[256,1024]{1,0:T(8,128)(2,1)}), bf16[1024,1024]{1,0:T(8,128)(2,1)}) %all-gather.27.cloned.1.call-update) | async-done | bytes 2097168 | tf_op jit(solution)/shard_map/all_gather | solution.py:247
  273.3 5.9 convert_bitcast_fusion.g_ref
  279.2 143.6 %all-gather.21.cloned.1.call-done = bf16[1024,4096]{1,0:T(8,128)(2,1)} async-done(((bf16[256,4096]{1,0:T(8,128)(2,1)}), bf16[1024,4096]{1,0:T(8,128)(2,1)}) %all-gather.21.cloned.1.call-update) | async-done | bytes 8388624 | tf_op jit(solution)/shard_map/all_gather | solution.py:247
  422.8 48.2 %multiply_convert_fusion = (bf16[1024,4096]{1,0:T(8,128)(2,1)}, f32[1024,4096]{1,0:T(8,128)}, f32[1024,4096]{1,0:T(8,128)}) fusion(f32[4096]{0:T(1024)S(1)} %bitcast.154, bf16[1024,1024]{1,0:T(8,128)(2,1)} %get-tuple-element.72, bf16[1024,4096]{1,0:T(8,128)(2,1)} %all-gather.21.cloned.1.call-done), kind=kOutput, calls=%fused_computation.12 | convolution fusion | flops 8866758656 | bytes 52445184 | tf_op jit(solution)/shard_map/dot_general | solution.py:327
  471.0 101.3 %all-gather.25.cloned.1.call-done = bf16[4096,1024]{1,0:T(8,128)(2,1)} async-done(((bf16[1024,1024]{1,0:T(8,128)(2,1)}), bf16[4096,1024]{1,0:T(8,128)(2,1)}) %all-gather.25.cloned.1.call-update) | async-done | bytes 8388624 | tf_op jit(solution)/shard_map/all_gather | solution.py:247
  572.2 25.9 %convert_reduce_fusion = (f32[4096]{0:T(1024)}, bf16[1024,4096]{1,0:T(8,128)(2,1)}) fusion(f32[1024,4096]{1,0:T(8,128)} %get-tuple-element.71, bf16[4096,1024]{1,0:T(8,128)(2,1)} %all-gather.25.cloned.1.call-done, bf16[1024,1024]{1,0:T(8,128)(2,1)} %bitcast.130, f32[1024,4096]{1,0:T(8,128)} %get-tuple-element.90, f32[4096]{0:T(1024)S(1)} %bitcast.155), kind=kOutput, calls=%fused_computation.11 | convolution fusion | flops 8661233664 | bytes 52461568 | tf_op jit(solution)/shard_map/dot_general | solution.py:337
  598.2 15.1 convolution_convert_fusion
  613.3 15.0 convolution_convert_fusion.1
  628.3 0.6 copy-done.29
  629.2 0.6 broadcast_in_dim.90.low_ref
  629.8 0.6 iota_add_fusion.top_ref
  630.4 5.8 negate_select_fusion
  636.2 223.3 %all-gather.17.cloned.1.call-done.k_ref.v_ref = bf16[2,2048,2048]{2,1,0:T(8,128)(2,1)} async-done(((bf16[2,512,2048]{2,1,0:T(8,128)(2,1)}), bf16[2,2048,2048]{2,1,0:T(8,128)(2,1)}) %all-gather.17.cloned.1.call-update) | async-done | bytes 16777232 | tf_op jit(solution)/shard_map/all_gather | solution.py:320
  859.4 72.8 %attention_both_ways.3 = (bf16[512,1024]{1,0:T(8,128)(2,1)}, bf16[512,1024]{1,0:T(8,128)(2,1)}, bf16[2048,1024]{1,0:T(8,128)(2,1)}, bf16[2048,1024]{1,0:T(8,128)(2,1)}) custom-call(bf16[1024,1024]{1,0:T(8,128)(2,1)} %copy-done.3, bf16[2,2048,2048]{2,1,0:T(8,128)(2,1)} %all-gather.17.cloned.1.call-done.k_ref.v_ref, ...), custom_call_target="tpu_custom_call" | custom-call | flops 99999997952 | bytes 20971520 | tf_op jit(solution)/shard_map/attention_both_ways/pallas_call | solution.py:199
  932.3 0.7 reduce-scatter.19.cloned.1.call-update
  933.0 73.3 %attention_both_ways.2 = (bf16[512,1024]{1,0:T(8,128)(2,1)}, bf16[512,1024]{1,0:T(8,128)(2,1)}, bf16[2048,1024]{1,0:T(8,128)(2,1)}, bf16[2048,1024]{1,0:T(8,128)(2,1)}) custom-call(bf16[1024,1024]{1,0:T(8,128)(2,1)} %copy-done.3, bf16[2,2048,2048]{2,1,0:T(8,128)(2,1)} %all-gather.17.cloned.1.call-done.k_ref.v_ref, ...), custom_call_target="tpu_custom_call" | custom-call | flops 99999997952 | bytes 20971520 | tf_op jit(solution)/shard_map/attention_both_ways/pallas_call | solution.py:199
  1006.4 0.7 reduce-scatter.17.cloned.1.call-update
  1007.7 1.3 constant_dynamic-update-slice_fusion.1
  1009.1 1.3 copy-done.13
  1010.4 5.4 convolution_convert_fusion.3
  1016.5 29.7 %reduce-scatter.15.cloned.1.call-done = bf16[512,1024]{1,0:T(8,128)(2,1)} async-done(((bf16[2048,1024]{1,0:T(8,128)(2,1)}), bf16[512,1024]{1,0:T(8,128)(2,1)}) %reduce-scatter.15.cloned.1.call-update) | async-done | bytes 1048592 | tf_op jit(solution)/shard_map/reduce_scatter | solution.py:355
  1046.2 80.3 %reduce-scatter.19.cloned.1.call-done = bf16[512,1024]{1,0:T(8,128)(2,1)} async-done(((bf16[2048,1024]{1,0:T(8,128)(2,1)}), bf16[512,1024]{1,0:T(8,128)(2,1)}) %reduce-scatter.19.cloned.1.call-update) | async-done | bytes 1048592 | tf_op jit(solution)/shard_map/reduce_scatter | solution.py:356
  1126.5 80.0 %reduce-scatter.13.cloned.1.call-done = bf16[512,1024]{1,0:T(8,128)(2,1)} async-done(((bf16[2048,1024]{1,0:T(8,128)(2,1)}), bf16[512,1024]{1,0:T(8,128)(2,1)}) %reduce-scatter.13.cloned.1.call-update) | async-done | bytes 1048592 | tf_op jit(solution)/shard_map/reduce_scatter | solution.py:355
  1206.5 80.3 %reduce-scatter.17.cloned.1.call-done = bf16[512,1024]{1,0:T(8,128)(2,1)} async-done(((bf16[2048,1024]{1,0:T(8,128)(2,1)}), bf16[512,1024]{1,0:T(8,128)(2,1)}) %reduce-scatter.17.cloned.1.call-update) | async-done | bytes 1048592 | tf_op jit(solution)/shard_map/reduce_scatter | solution.py:356
  1286.8 11.4 convert_reduce_fusion.1
  1298.2 2.9 copy-done.9
  1301.1 8.8 convolution_convert_fusion.2
  1310.0 86.5 %reduce-scatter.29.cloned.1.call-done = bf16[64,4096]{1,0:T(8,128)(2,1)} async-done(((bf16[1024,4096]{1,0:T(8,128)(2,1)}), bf16[64,4096]{1,0:T(8,128)(2,1)}) %reduce-scatter.29.cloned.1.call-update) | async-done | bytes 524304 | tf_op jit(solution)/shard_map/reduce_scatter | solution.py:251
  1396.5 65.4 %reduce-scatter.25.cloned.1.call-done = bf16[64,1024]{1,0:T(8,128)(2,1)} async-done(((bf16[1024,1024]{1,0:T(8,128)(2,1)}), bf16[64,1024]{1,0:T(8,128)(2,1)}) %reduce-scatter.25.cloned.1.call-update) | async-done | bytes 131088 | tf_op jit(solution)/shard_map/reduce_scatter | solution.py:251
  1462.0 15.7 reduce-scatter.35.cloned.1.call-done
  1477.7 89.5 %reduce-scatter.21.cloned.1.call-done = bf16[64,3072]{1,0:T(8,128)(2,1)} async-done(((bf16[1024,3072]{1,0:T(8,128)(2,1)}), bf16[64,3072]{1,0:T(8,128)(2,1)}) %reduce-scatter.21.cloned.1.call-update) | async-done | bytes 393232 | tf_op jit(solution)/shard_map/reduce_scatter | solution.py:251
  1567.3 15.9 reduce-scatter.31.cloned.1.call-done
  1583.8 15.4 fusion.69
  1599.2 2.3 fusion.68
  1601.5 15.0 fusion.39
  1616.6 31.8 %all-gather.35.cloned.1.call-done = bf16[4096,512]{1,0:T(8,128)(2,1)} async-done(((bf16[256,512]{1,0:T(8,128)(2,1)}), bf16[4096,512]{1,0:T(8,128)(2,1)}) %all-gather.35.cloned.1.call-update) | async-done | bytes 4194320 | tf_op jit(solution)/shard_map/all_gather | solution.py:253
  1648.4 21.1 %multiply_subtract_fusion = (f32[4096,512]{1,0:T(8,128)}, f32[4096,512]{1,0:T(8,128)}, f32[4096,512]{1,0:T(8,128)}) fusion(f32[4096,512]{1,0:T(8,128)} %param.30, bf16[4096,512]{1,0:T(8,128)(2,1)} %all-gather.35.cloned.1.call-done, f32[4096,512]{1,0:T(8,128)} %param.31, f32[4096,512]{1,0:T(8,128)} %param.32), kind=kLoop, calls=%fused_computation.36 | loop fusion | flops 33554432 | bytes 54525952 | tf_op jit(solution)/shard_map/sub | solution.py:261
  1669.6 45.7 %all-gather.33.cloned.1.call-done = bf16[1024,2048]{1,0:T(8,128)(2,1)} async-done(((bf16[64,2048]{1,0:T(8,128)(2,1)}), bf16[1024,2048]{1,0:T(8,128)(2,1)}) %all-gather.33.cloned.1.call-update) | async-done | bytes 4194320 | tf_op jit(solution)/shard_map/all_gather | solution.py:253
  1715.3 20.2 %multiply_subtract_fusion.1 = (f32[1024,2048]{1,0:T(8,128)}, f32[1024,2048]{1,0:T(8,128)}, f32[1024,2048]{1,0:T(8,128)}) fusion(f32[1024,2048]{1,0:T(8,128)} %param.27, bf16[1024,2048]{1,0:T(8,128)(2,1)} %all-gather.33.cloned.1.call-done, f32[1024,2048]{1,0:T(8,128)} %param.28, f32[1024,2048]{1,0:T(8,128)} %param.29), kind=kLoop, calls=%fused_computation.37 | loop fusion | flops 33554432 | bytes 54525952 | tf_op jit(solution)/shard_map/sub | solution.py:261
  1735.5 18.7 %all-gather.31.cloned.1.call-done = bf16[1024,512]{1,0:T(8,128)(2,1)} async-done(((bf16[64,512]{1,0:T(8,128)(2,1)}), bf16[1024,512]{1,0:T(8,128)(2,1)}) %all-gather.31.cloned.1.call-update) | async-done | bytes 1048592 | tf_op jit(solution)/shard_map/all_gather | solution.py:253
  1754.2 7.0 multiply_subtract_fusion.3
  1761.2 12.7 fusion.56
  1774.1 4.0 fusion.33
  1778.2 39.6 %psum.7 = f32[13,1024]{1,0:T(8,128)S(1)} all-reduce(f32[13,1024]{1,0:T(8,128)S(1)} %concatenate.23), channel_id=1, replica_groups=mesh['batch'=4,'group'=2,'ctx'=4] {'batch','group','ctx'}, use_global_device_ids=true, to_apply=%region_26.27 | all-reduce | flops 13312 | bytes 106496 | tf_op jit(solution)/shard_map/psum | solution.py:405
  1817.8 0.7 multiply_subtract_fusion.4
  1818.5 6.7 add_add_fusion.2
  1825.2 15.2 multiply_subtract_fusion.2
  (151 shorter events, 3.9 us)
Async XLA Ops:
  7.2 32.9 %all-gather.13.cloned.1.call-start = ((), (), s32[]{:S(2)}) async-start(), calls=%async_computation.12 | async-start | bytes 2359296 | tf_op jit(solution)/shard_map/all_gather | solution.py:246
  9.6 65.7 %all-gather.19.cloned.1.call-start = ((), (), s32[]{:S(2)}) async-start(), calls=%async_computation.15 | async-start | bytes 3145728 | tf_op jit(solution)/shard_map/all_gather | solution.py:246
  12.4 98.3 %copy-start.15 = (f32[13,512]{1,0:T(8,128)S(1)}, f32[13,512]{1,0:T(8,128)}, u32[]{:S(2)}) copy-start(f32[13,512]{1,0:T(8,128)} %param.33) | copy-start | bytes 79876
  12.4 98.3 %copy-start.4 = (bf16[2,512,1024]{2,1,0:T(8,128)(2,1)S(1)}, bf16[2,512,1024]{2,1,0:T(8,128)(2,1)}, u32[]{:S(2)}) copy-start(bf16[2,512,1024]{2,1,0:T(8,128)(2,1)} %param.18) | copy-start | bytes 6291460
  12.4 98.2 %all-gather.23.cloned.1.call-start = ((), (), s32[]{:S(2)}) async-start(), calls=%async_computation.17 | async-start | bytes 3145728 | tf_op jit(solution)/shard_map/all_gather | solution.py:246
  15.3 212.1 %all-gather.15.cloned.1.call-start = ((), (), s32[]{:S(2)}) async-start(), calls=%async_computation.13 | async-start | bytes 7864320 | tf_op jit(solution)/shard_map/all_gather | solution.py:247
  40.1 233.2 %all-gather.27.cloned.1.call-start = ((), (), s32[]{:S(2)}) async-start(), calls=%async_computation.19 | async-start | bytes 2621440 | tf_op jit(solution)/shard_map/all_gather | solution.py:247
  50.1 372.7 %all-gather.21.cloned.1.call-start = ((), (), s32[]{:S(2)}) async-start(), calls=%async_computation.16 | async-start | bytes 10485760 | tf_op jit(solution)/shard_map/all_gather | solution.py:247
  75.4 496.9 %all-gather.25.cloned.1.call-start = ((), (), s32[]{:S(2)}) async-start(), calls=%async_computation.18 | async-start | bytes 10485760 | tf_op jit(solution)/shard_map/all_gather | solution.py:247
  110.7 748.8 %all-gather.17.cloned.1.call-start = ((), (), s32[]{:S(2)}) async-start(), calls=%async_computation.14 | async-start | bytes 20971520 | tf_op jit(solution)/shard_map/all_gather | solution.py:320
  111.8 4.5 copy-start.25
  111.8 133.7 %copy-start.21 = (f32[1024]{0:T(1024)}, f32[1024]{0:T(1024)S(1)}, u32[]{:S(2)}) copy-start(f32[1024]{0:T(1024)S(1)} %rsqrt.13) | copy-start | bytes 12292
  111.8 133.7 %copy-start.23 = (f32[1,4,2,128]{3,1,2,0:T(4,128)}, f32[1,4,2,128]{3,1,2,0:T(4,128)S(1)}, u32[]{:S(2)}) copy-start(f32[1,4,2,128]{3,1,2,0:T(4,128)S(1)} %copy.37) | copy-start | bytes 12292
  116.3 1.7 copy-start.33
  116.4 1.7 copy-start.35
  116.4 1.7 copy-start.37
  117.0 1.1 copy-start.17
  117.0 1.1 copy-start.19
  118.0 127.5 %copy-start.1 = (f32[512,128]{1,0:T(8,128)}, f32[512,128]{1,0:T(8,128)S(1)}, u32[]{:S(2)}) copy-start(f32[512,128]{1,0:T(8,128)S(1)} %get-tuple-element.88.sin_ref.sinq_ref) | copy-start | bytes 786436
  118.1 127.5 %copy-start.2 = (f32[512,128]{1,0:T(8,128)}, f32[512,128]{1,0:T(8,128)S(1)}, u32[]{:S(2)}) copy-start(f32[512,128]{1,0:T(8,128)S(1)} %get-tuple-element.89.cos_ref.cosq_ref) | copy-start | bytes 786436
  245.6 2.0 copy-start
  247.6 1.3 copy-start.3
  248.9 767.0 %reduce-scatter.33.cloned.1.call-start = ((), (), s32[]{:S(2)}) async-start(), calls=%async_computation.33 | async-start | bytes 8912896 | tf_op jit(solution)/shard_map/reduce_scatter | solution.py:251
  572.2 25.9 %copy-start.10 = (bf16[1024,1024]{1,0:T(8,128)(2,1)S(1)}, bf16[1024,1024]{1,0:T(8,128)(2,1)}, u32[]{:S(2)}) copy-start(bf16[1024,1024]{1,0:T(8,128)(2,1)} %get-tuple-element.72) | copy-start | bytes 6291460
  628.2 0.7 copy-start.29
  628.2 2.1 copy-start.34
  628.3 2.1 copy-start.36
  628.3 2.1 copy-start.38
  628.3 417.9 %reduce-scatter.15.cloned.1.call-start = ((), (), s32[]{:S(2)}) async-start(), calls=%async_computation.21 | async-start | bytes 5242880 | tf_op jit(solution)/shard_map/reduce_scatter | solution.py:355
  932.3 194.2 %reduce-scatter.19.cloned.1.call-start = ((), (), s32[]{:S(2)}) async-start(), calls=%async_computation.23 | async-start | bytes 5242880 | tf_op jit(solution)/shard_map/reduce_scatter | solution.py:356
  933.0 273.5 %reduce-scatter.13.cloned.1.call-start = ((), (), s32[]{:S(2)}) async-start(), calls=%async_computation.20 | async-start | bytes 5242880 | tf_op jit(solution)/shard_map/reduce_scatter | solution.py:355
  1006.3 280.4 %reduce-scatter.17.cloned.1.call-start = ((), (), s32[]{:S(2)}) async-start(), calls=%async_computation.22 | async-start | bytes 5242880 | tf_op jit(solution)/shard_map/reduce_scatter | solution.py:356
  1007.1 1.9 copy-start.12
  1007.1 389.3 %reduce-scatter.29.cloned.1.call-start = ((), (), s32[]{:S(2)}) async-start(), calls=%async_computation.30 | async-start | bytes 8912896 | tf_op jit(solution)/shard_map/reduce_scatter | solution.py:251
  1007.7 454.3 %reduce-scatter.25.cloned.1.call-start = ((), (), s32[]{:S(2)}) async-start(), calls=%async_computation.27 | async-start | bytes 2228224 | tf_op jit(solution)/shard_map/reduce_scatter | solution.py:251
  1009.1 1.3 copy-start.13
  1010.4 276.4 %copy-start.11 = (bf16[512,1024]{1,0:T(8,128)(2,1)S(1)}, bf16[512,1024]{1,0:T(8,128)(2,1)}, u32[]{:S(2)}) copy-start(bf16[512,1024]{1,0:T(8,128)(2,1)} %get-tuple-element.36) | copy-start | bytes 3145732
  1015.9 461.8 %reduce-scatter.35.cloned.1.call-start = ((), (), s32[]{:S(2)}) async-start(), calls=%async_computation.34 | async-start | bytes 786432 | tf_op jit(solution)/shard_map/reduce_scatter | solution.py:252
  1016.5 550.8 %reduce-scatter.21.cloned.1.call-start = ((), (), s32[]{:S(2)}) async-start(), calls=%async_computation.24 | async-start | bytes 6684672 | tf_op jit(solution)/shard_map/reduce_scatter | solution.py:251
  1298.2 2.9 copy-start.9
  1309.9 273.5 %copy-start.8 = (bf16[2,512,1024]{2,1,0:T(8,128)(2,1)S(1)}, bf16[2,512,1024]{2,1,0:T(8,128)(2,1)}, u32[]{:S(2)}) copy-start(bf16[2,512,1024]{2,1,0:T(8,128)(2,1)} %param.20) | copy-start | bytes 6291460
  1309.9 273.9 %copy-start.30 = (f32[4096]{0:T(1024)S(1)}, f32[4096]{0:T(1024)}, u32[]{:S(2)}) copy-start(f32[4096]{0:T(1024)} %get-tuple-element.92) | copy-start | bytes 49156
  1309.9 273.4 %reduce-scatter.31.cloned.1.call-start = ((), (), s32[]{:S(2)}) async-start(), calls=%async_computation.31 | async-start | bytes 786432 | tf_op jit(solution)/shard_map/reduce_scatter | solution.py:252
  1396.4 220.1 %reduce-scatter.27.cloned.1.call-start = ((), (), s32[]{:S(2)}) async-start(), calls=%async_computation.28 | async-start | bytes 196608 | tf_op jit(solution)/shard_map/reduce_scatter | solution.py:252
  1461.9 186.5 %all-gather.35.cloned.1.call-start = ((), (), s32[]{:S(2)}) async-start(), calls=%async_computation.35 | async-start | bytes 4456448 | tf_op jit(solution)/shard_map/all_gather | solution.py:253
  1477.7 191.9 %reduce-scatter.23.cloned.1.call-start = ((), (), s32[]{:S(2)}) async-start(), calls=%async_computation.25 | async-start | bytes 589824 | tf_op jit(solution)/shard_map/reduce_scatter | solution.py:252
  1567.3 148.0 %all-gather.33.cloned.1.call-start = ((), (), s32[]{:S(2)}) async-start(), calls=%async_computation.32 | async-start | bytes 4456448 | tf_op jit(solution)/shard_map/all_gather | solution.py:253
  1583.3 170.9 %all-gather.31.cloned.1.call-start = ((), (), s32[]{:S(2)}) async-start(), calls=%async_computation.29 | async-start | bytes 1114112 | tf_op jit(solution)/shard_map/all_gather | solution.py:253
  1583.8 15.4 copy-start.14
  1583.8 15.4 copy-start.39
  1599.1 2.4 copy-start.5
  1599.1 2.4 copy-start.31
  1599.2 2.4 copy-start.32
  1616.6 208.7 %all-gather.29.cloned.1.call-start = ((), (), s32[]{:S(2)}) async-start(), calls=%async_computation.26 | async-start | bytes 3342336 | tf_op jit(solution)/shard_map/all_gather | solution.py:253
  1735.4 25.7 %copy-start.18 = (f32[1,1024]{1,0:T(1,128)S(1)}, f32[1,1024]{1,0:T(1,128)}, u32[]{:S(2)}) copy-start(f32[1,1024]{1,0:T(1,128)} %copy-done.17) | copy-start | bytes 12292
  1735.5 25.7 %copy-start.20 = (f32[1,1024]{1,0:T(1,128)S(1)}, f32[1,1024]{1,0:T(1,128)}, u32[]{:S(2)}) copy-start(f32[1,1024]{1,0:T(1,128)} %copy-done.19) | copy-start | bytes 12292
  1735.5 25.7 %copy-start.24 = (f32[1,4,2,128]{3,1,2,0:T(4,128)S(1)}, f32[1,4,2,128]{3,1,2,0:T(4,128)}, u32[]{:S(2)}) copy-start(f32[1,4,2,128]{3,1,2,0:T(4,128)} %copy-done.23) | copy-start | bytes 12292
  1761.2 12.8 copy-start.26
  1761.2 12.8 copy-start.6
  1761.2 12.8 copy-start.22
  1774.0 4.1 copy-start.7
  1774.0 43.8 %copy-start.16 = (f32[13,512]{1,0:T(8,128)S(1)}, f32[13,512]{1,0:T(8,128)}, u32[]{:S(2)}) copy-start(f32[13,512]{1,0:T(8,128)} %param.33) | copy-start | bytes 79876
  1774.0 43.8 %copy-start.27 = (f32[13,512]{1,0:T(8,128)S(1)}, f32[13,512]{1,0:T(8,128)}, u32[]{:S(2)}) copy-start(f32[13,512]{1,0:T(8,128)} %param.34) | copy-start | bytes 79876
  1774.0 43.8 %copy-start.28 = (f32[13,512]{1,0:T(8,128)S(1)}, f32[13,512]{1,0:T(8,128)}, u32[]{:S(2)}) copy-start(f32[13,512]{1,0:T(8,128)} %param.35) | copy-start | bytes 79876
Sparse Core Ops, SparseCore 0:
  10.1 29.8 all-gather.12
  42.2 33.1 all-gather.18
  77.5 33.1 all-gather.22
  112.1 115.3 all-gather.14
  228.9 44.3 all-gather.26
  274.7 148.0 all-gather.20
  424.3 147.8 all-gather.24
  574.4 284.9 all-gather.16
  864.1 102.8 reduce-scatter.32
  969.7 76.5 reduce-scatter.14
  1049.2 77.2 reduce-scatter.18
  1129.2 77.2 reduce-scatter.12
  1209.5 77.2 reduce-scatter.16
  1291.3 105.1 reduce-scatter.28
  1400.6 61.2 reduce-scatter.24
  1464.1 13.5 reduce-scatter.34
  1482.0 85.2 reduce-scatter.20
  1569.5 13.7 reduce-scatter.30
  1585.5 10.2 reduce-scatter.26
  1597.8 50.5 all-gather.34
  1650.7 11.5 reduce-scatter.22
  1664.7 50.5 all-gather.32
  1717.7 36.4 all-gather.30
  1756.6 44.8 all-gather.28
